TPU v7x, 32 devices: a whole 2x2x4 slice. The times are simulated.
32 devices in a mesh: group: 2 (over y), ctx: 16 (over z, x, core).
Axes of the slice: x: 2, y: 2, z: 4, core: 2. Of those that a mesh axis runs over, the one named last changes fastest.
Arguments:
- queries: bfloat16 [2048, 64, 320], P(('group', 'ctx')), parts along dimension 0, may hold values from -32 to 32
- latent_keys: bfloat16 [2048, 320], P(('group', 'ctx')), parts along dimension 0, may hold values from -4 to 4
- hidden: bfloat16 [2048, 3584], P(('group', 'ctx')), parts along dimension 0, may hold values from -6 to 6
- routes: int32 [2048, 2], P(('group', 'ctx')), parts along dimension 0, may hold values from 0 to 3, all different within a row; in each aligned block of 64 rows (0 to 63, 64 to 127, ...) at most 40 rows name the same one
- route_weights: float32 [2048, 2], P(('group', 'ctx')), parts along dimension 0, may hold values from 0.05 to 0.5
- w_gate: bfloat16 [16, 3584, 256], P('ctx'), may hold values from -0.09375 to 0.09375
- w_up: bfloat16 [16, 3584, 256], P('ctx'), may hold values from -0.09375 to 0.09375
- w_down: bfloat16 [16, 256, 3584], P('ctx'), may hold values from -0.1875 to 0.1875
Outputs:
- attended: bfloat16 [2048, 64, 256], P(('group', 'ctx')), parts along dimension 0
- mixed: bfloat16 [2048, 3584], P(('group', 'ctx')), parts along dimension 0
There are 2 independent parts, one for each index of `group`. A program takes and returns all parts, laid end to end along the dimension named above; an argument that names none is the same for every part. Nothing has to cross between parts.
Inputs may be any that keep to these rules, and one draw needn't show every extreme that they name: `routes`: each row names 2 different experts; among the rows of one device no expert is named more than 40 times, a bound that some block reaches.
All inputs are finite; a program needn't handle non-finite values.
Results may differ from a plain program's by a relative error of at most 0.0059.
Values may be sent and summed in bfloat16 or wider, within the bound.
A program may use at most 128 MiB of HBM per device.

v0:
```python
import math

import jax
import jax.numpy as jnp
from jax import lax
from jax.sharding import PartitionSpec as P

LAT = 256
ROPE = 64
NOPE_DIM = 128
D = 3584
SPLIT = 4
TOPK = 2


def attention_part(queries, latent_keys):
    tok_rows, heads, width = queries.shape
    score_scale = 1.0 / math.sqrt(NOPE_DIM + ROPE)
    first_query = lax.axis_index("ctx") * tok_rows
    last_query = first_query + tok_rows - 1
    row_total = tok_rows * heads
    flat_queries = queries.reshape(row_total, width)
    query_pos = first_query + jnp.arange(row_total, dtype=jnp.int32) // heads
    buffer_rows = 512
    far_away = 1 << 30

    def update(attention, block_keys, key_pos):
        run_max, run_sum, accum = attention
        scores = (
            lax.dot_general(
                flat_queries,
                block_keys,
                (((1,), (1,)), ((), ())),
                preferred_element_type=jnp.float32,
            )
            * score_scale
        )
        scores = jnp.where(key_pos[None, :] <= query_pos[:, None], scores, -jnp.inf)
        new_max = jnp.maximum(run_max, jnp.max(scores, axis=1, keepdims=True))
        expo = jnp.exp(scores - new_max)
        factor = jnp.exp(run_max - new_max)
        new_sum = run_sum * factor + jnp.sum(expo, axis=1, keepdims=True)
        product = jnp.dot(
            expo.astype(jnp.bfloat16), block_keys[:, :LAT], preferred_element_type=jnp.float32
        )
        return (new_max, new_sum, accum * factor + product)

    attention = (
        jnp.full((row_total, 1), -1e30, jnp.float32),
        jnp.zeros((row_total, 1), jnp.float32),
        jnp.zeros((row_total, LAT), jnp.float32),
    )
    piece = lax.all_gather(latent_keys, "ctx", axis=0, tiled=True)
    piece_rows = piece.shape[0]
    attention, fold_buffer, fold_buf_pos, filled = (
        attention,
        jnp.zeros((buffer_rows, width), jnp.bfloat16),
        jnp.full((buffer_rows,), far_away, jnp.int32),
        jnp.zeros((), jnp.int32),
    )

    def one_block(index, held):
        block_start = index * buffer_rows
        block_keys = lax.dynamic_slice_in_dim(piece, index * buffer_rows, buffer_rows, 0)
        key_pos = block_start + jnp.arange(buffer_rows, dtype=jnp.int32)
        return lax.cond(
            block_start <= last_query,
            lambda kept: update(kept, block_keys, key_pos),
            lambda kept: kept,
            held,
        )

    attention = lax.fori_loop(0, piece_rows // buffer_rows, one_block, attention)
    attention, buffer, buf_pos, filled = (attention, fold_buffer, fold_buf_pos, filled)
    attention = lax.cond(
        filled > 0, lambda kept: update(kept, buffer, buf_pos), lambda kept: kept, attention
    )
    run_max, run_sum, accum = attention
    return (accum / run_sum).astype(jnp.bfloat16).reshape(tok_rows, heads, LAT)


def expert_part(hidden, routes, route_weights, w_gate, w_up, w_down):
    tok_rows = hidden.shape[0]
    ctx_count = lax.axis_size("ctx")
    expert_span = SPLIT
    expert_count = ctx_count // SPLIT
    most_slots = tok_rows * TOPK * 5 // (4 * expert_count)
    flat_ids = routes.reshape(-1)
    onehot = (flat_ids[:, None] == jnp.arange(expert_count, dtype=jnp.int32)[None, :]).astype(
        jnp.int32
    )
    rank = jnp.sum((jnp.cumsum(onehot, axis=0) - onehot) * onehot, axis=1)
    slot = flat_ids * most_slots + rank
    table_rows = expert_count * most_slots
    matches = slot[None, :] == jnp.arange(table_rows, dtype=jnp.int32)[:, None]
    selector = jnp.sum(
        matches.reshape(table_rows, tok_rows, TOPK).astype(jnp.int32), axis=2
    ).astype(jnp.bfloat16)
    per_expert = (
        jnp.dot(selector, hidden, preferred_element_type=jnp.float32)
        .astype(jnp.bfloat16)
        .reshape(expert_count, most_slots, D)
    )
    outgoing = jnp.repeat(per_expert, expert_span, axis=0)
    arrived = lax.all_to_all(outgoing, "ctx", split_axis=0, concat_axis=0, tiled=True)
    token_block = arrived.reshape(ctx_count * most_slots, D)
    gate = jnp.dot(token_block, w_gate[0], preferred_element_type=jnp.float32)
    upper = jnp.dot(token_block, w_up[0], preferred_element_type=jnp.float32)
    units = (jax.nn.silu(gate) * upper).astype(jnp.bfloat16)
    partial_value = (
        jnp.dot(units, w_down[0], preferred_element_type=jnp.float32)
        .astype(jnp.bfloat16)
        .reshape(ctx_count, most_slots, D)
    )
    returned = lax.all_to_all(partial_value, "ctx", split_axis=0, concat_axis=0, tiled=True)
    summed = jnp.sum(
        returned.reshape(expert_count, expert_span, most_slots, D).astype(jnp.float32), axis=1
    ).reshape(table_rows, D)
    slot_grid = slot.reshape(tok_rows, TOPK)
    combine = jnp.sum(
        (slot_grid[:, :, None] == jnp.arange(table_rows, dtype=jnp.int32)[None, None, :]).astype(
            jnp.float32
        )
        * route_weights[:, :, None],
        axis=1,
    )
    mixed = jnp.dot(
        combine, summed, preferred_element_type=jnp.float32, precision=lax.Precision.HIGHEST
    )
    return mixed.astype(jnp.bfloat16)


def per_device(queries, latent_keys, hidden, routes, route_weights, w_gate, w_up, w_down):
    attended = attention_part(queries, latent_keys)
    mixed = expert_part(hidden, routes, route_weights, w_gate, w_up, w_down)
    return (attended, mixed)


def solution(mesh):
    in_specs = (
        P(("group", "ctx"), None, None),
        P(("group", "ctx"), None),
        P(("group", "ctx"), None),
        P(("group", "ctx"), None),
        P(("group", "ctx"), None),
        P("ctx", None, None),
        P("ctx", None, None),
        P("ctx", None, None),
    )
    out_specs = (P(("group", "ctx"), None, None), P(("group", "ctx"), None))
    return jax.shard_map(
        per_device, mesh=mesh, in_specs=in_specs, out_specs=out_specs, check_vma=False
    )
```

profile of v0, /device:TPU:17, one launch (start us, length us, event | category | flops | bytes accessed | tf_op | source)
XLA Modules:
  0.0 278.3 jit_solution(13836153592036404977)
XLA Ops:
  0.6 0.9 copy.23
  1.5 0.1 eq.42
  1.8 0.2 reduce_window_sum.11
  2.0 0.2 select_reduce_fusion.1
  2.1 0.1 reduce_sum.54
  2.4 0.7 multiply_add_fusion.1
  3.1 1.5 convolution_convert_fusion.1
  4.6 0.3 broadcast_in_dim.34
  5.0 106.8 %all_to_all.10 = bf16[16,40,3584]{2,1,0:T(8,128)(2,1)S(1)} all-to-all(bf16[16,40,3584]{2,1,0:T(8,128)(2,1)S(1)} %bitcast.43), channel_id=1, replica_groups=mesh['group'=2,'ctx'=16] {'ctx'}, dimensions={0} | all-to-all | bytes 9175040 | tf_op jit(solution)/shard_map/all_to_all | solution.py:105
  111.7 2.1 copy-done.3
  113.9 1.3 fusion.15
  115.3 9.8 %convolution_convert_fusion = bf16[640,3584]{1,0:T(8,128)(2,1)} fusion(bf16[1,256,3584]{2,1,0:T(8,128)(2,1)S(1)} %copy-done, bf16[640,3584]{1,0:T(8,128)(2,1)} %bitcast.50, bf16[1,3584,256]{2,1,0:T(8,128)(2,1)} %param.18, f32[640,256]{1,0:T(8,128)S(1)} %fusion.15), kind=kOutput, calls=%fused_computation.21 | convolution fusion | flops 2352087040 | bytes 13500416 | tf_op jit(solution)/shard_map/dot_general | solution.py:111
  125.1 5.8 %all-to-all-start.1 = ((bf16[16,40,3584]{2,1,0:T(8,128)(2,1)}), bf16[16,40,3584]{2,1,0:T(8,128)(2,1)}, u32[]{:S(2)}, u32[]{:S(2)}) async-start(bf16[16,40,3584]{2,1,0:T(8,128)(2,1)} %bitcast.48), calls=%async_computation.1 | async-start | bytes 9175040 | tf_op jit(solution)/shard_map/all_to_all | solution.py:115
  130.9 0.1 select_reduce_fusion
  131.0 113.9 %all_gather.3 = bf16[1024,320]{1,0:T(8,128)(2,1)S(1)} all-gather(bf16[64,320]{1,0:T(8,128)(2,1)S(1)} %copy-done.4), channel_id=1, replica_groups=mesh['group'=2,'ctx'=16] {'ctx'}, dimensions={0}, use_global_device_ids=true | all-gather | bytes 696320 | tf_op jit(solution)/shard_map/all_gather | solution.py:53
  244.9 2.3 broadcast.51
  247.2 22.1 %while.18 = (s32[]{:T(128)}, f32[4096,1]{0,1:T(1,128)S(1)}, f32[4096,1]{0,1:T(1,128)S(1)}, f32[4096,256]{1,0:T(8,128)}, s32[]{:T(128)}, /*index=5*/bf16[1024,320...) while((s32[]{:T(128)}, f32[4096,1]{0,1:T(1,128)S(1)}, ...), condition=%wide.region_5.6_spmd.clone, body=%wide.region_0.5_spmd.clone.sunk | while | flops 2434839040 | bytes 70787480 | solution.py:73
  247.3 11.1 %conditional.3 = ((f32[4096,1]{0,1:T(1,128)S(1)}, f32[4096,1]{0,1:T(1,128)S(1)}, f32[4096,256]{1,0:T(8,128)})) conditional(s32[]{:T(128)} %convert_element_type.73, (f32[4096,1]{0,1:T(1,128)S(1)}, f32[4096,1]{0,1:T(1,128)S(1)}, f32[4096,256]{1,0:T(8,128)}) %tuple.65, (s32[]{:T(128)}, s32[512]{0:T(512)S(1)}, s32[]{:T(128)}, ...), branch_computations={%region_1.1_spmd, %region_2.4_spmd.clone} | conditional | flops 2434834944 | bytes 70752400 | solution.py:66
  247.3 4.3 %fusion.34 = (f32[4096]{0:T(1024)S(1)}, f32[4096,512]{0,1:T(8,128)S(1)}) fusion(bf16[4096,320]{1,0:T(8,128)(2,1)} %get-tuple-element.294, bf16[1024,320]{1,0:T(8,128)(2,1)S(1)} %get-tuple-element.293, s32[]{:T(128)S(6)} %select_n.27, s32[4096]{0:T(1024)S(1)} %fusion.8, s32[512]{0:T(512)S(1)} %broadcast_add_fusion), kind=kOutput, calls=%fused_computation.48 | convolution fusion | flops 1350561792 | bytes 11438084 | tf_op jit(solution)/shard_map/while/body/eval_jaxpr/cond/branch_1_fun/dot_general | solution.py:30
  251.7 1.3 fusion.3
  253.1 0.8 copy-done.1
  253.9 2.4 convolution_add_fusion
  256.3 2.0 copy-done.2
  258.3 11.0 %conditional.3 = ((f32[4096,1]{0,1:T(1,128)S(1)}, f32[4096,1]{0,1:T(1,128)S(1)}, f32[4096,256]{1,0:T(8,128)})) conditional(s32[]{:T(128)} %convert_element_type.73, (f32[4096,1]{0,1:T(1,128)S(1)}, f32[4096,1]{0,1:T(1,128)S(1)}, f32[4096,256]{1,0:T(8,128)}) %tuple.65, (s32[]{:T(128)}, s32[512]{0:T(512)S(1)}, s32[]{:T(128)}, ...), branch_computations={%region_1.1_spmd, %region_2.4_spmd.clone} | conditional | flops 2434834944 | bytes 70752400 | solution.py:66
  258.4 4.3 %fusion.34 = (f32[4096]{0:T(1024)S(1)}, f32[4096,512]{0,1:T(8,128)S(1)}) fusion(bf16[4096,320]{1,0:T(8,128)(2,1)} %get-tuple-element.294, bf16[1024,320]{1,0:T(8,128)(2,1)S(1)} %get-tuple-element.293, s32[]{:T(128)S(6)} %select_n.27, s32[4096]{0:T(1024)S(1)} %fusion.8, s32[512]{0:T(512)S(1)} %broadcast_add_fusion), kind=kOutput, calls=%fused_computation.48 | convolution fusion | flops 1350561792 | bytes 11438084 | tf_op jit(solution)/shard_map/while/body/eval_jaxpr/cond/branch_1_fun/dot_general | solution.py:30
  262.7 1.3 fusion.3
  264.1 0.8 copy-done.1
  264.9 2.4 convolution_add_fusion
  267.3 2.0 copy-done.2
  269.4 3.5 %divide_convert_fusion = bf16[4096,256]{1,0:T(8,128)(2,1)} fusion(f32[4096,256]{1,0:T(8,128)} %get-tuple-element.245, f32[4096]{0:T(1024)S(1)} %bitcast.54), kind=kLoop, calls=%fused_computation.24 | loop fusion | flops 2097152 | bytes 6307840 | tf_op jit(solution)/shard_map/convert_element_type | solution.py:79
  272.9 3.3 %convert_reduce_fusion = f32[4,40,3584]{2,1,0:T(8,128)S(1)} fusion(bf16[16,40,3584]{2,1,0:T(8,128)(2,1)} %all-to-all-done.1), kind=kLoop, calls=%fused_computation.20 | loop fusion | flops 4014080 | bytes 6881280 | tf_op jit(solution)/shard_map/reduce_sum | solution.py:116
  276.3 2.1 convolution_convert_fusion.2
  (35 shorter events, 0.5 us)
Async XLA Ops:
  0.6 114.6 %copy-start = (bf16[1,256,3584]{2,1,0:T(8,128)(2,1)S(1)}, bf16[1,256,3584]{2,1,0:T(8,128)(2,1)}, u32[]{:S(2)}) copy-start(bf16[1,256,3584]{2,1,0:T(8,128)(2,1)} %param.19) | copy-start | bytes 5505028
  5.0 108.9 %copy-start.6 = (bf16[1,3584,256]{2,1,0:T(8,128)(2,1)S(1)}, bf16[1,3584,256]{2,1,0:T(8,128)(2,1)}, u32[]{:S(2)}) copy-start(bf16[1,3584,256]{2,1,0:T(8,128)(2,1)} %param.17) | copy-start | bytes 5505028
  111.7 2.1 copy-start.3
  125.1 5.8 %copy-start.5 = (f32[64,2]{0,1:T(2,128)S(1)}, f32[64,2]{0,1:T(2,128)}, u32[]{:S(2)}) copy-start(f32[64,2]{0,1:T(2,128)} %param.16) | copy-start | bytes 1540
  125.1 5.9 %copy-start.4 = (bf16[64,320]{1,0:T(8,128)(2,1)S(1)}, bf16[64,320]{1,0:T(8,128)(2,1)}, u32[]{:S(2)}) copy-start(bf16[64,320]{1,0:T(8,128)(2,1)} %param.13) | copy-start | bytes 122884
  125.1 147.9 %all-to-all-start.1 = ((bf16[16,40,3584]{2,1,0:T(8,128)(2,1)}), bf16[16,40,3584]{2,1,0:T(8,128)(2,1)}, u32[]{:S(2)}, u32[]{:S(2)}) async-start(bf16[16,40,3584]{2,1,0:T(8,128)(2,1)} %bitcast.48), calls=%async_computation.1 | async-start | bytes 9175040 | tf_op jit(solution)/shard_map/all_to_all | solution.py:115
  251.7 2.2 copy-start.1
  256.3 2.0 copy-start.2
  262.7 2.2 copy-start.1
  267.3 2.0 copy-start.2
where the time goes:
time: 279 us; the launch traced here: 278 us
  blocking collectives  221 us (79%)
  matrix products  28.1 us (10%)
  local copies, waits for them, and re-layouts  11.7 us (4%)
  other arithmetic  11.1 us (4%)
  starting transfers between devices  5.8 us (2%)
    all_gather x1, blocking collectives, attention_part(): piece = lax.all_gather(latent_keys, 'ctx', axis=0, tiled=True)  114 us
    all_to_all x1, blocking collectives, expert_part(): lax.all_to_all(outgoing, 'ctx', split_axis=0, concat_axis=0, tiled=True)  107 us
    dot_general x1, matrix products, expert_part(): jnp.dot(units, w_down[0], preferred_element_type=jnp.float32)  9.8 us
    dot_general x2, matrix products, update(): lax.dot_general(flat_queries, block_keys, (((1,), (1,)), ((), ())), prefe...  8.65 us
    all_to_all x1, starting transfers between devices, expert_part(): lax.all_to_all(partial_value, 'ctx', split_axis=0, concat_axis=0, tiled=T...  5.8 us
    cond x10, local copies, waits for them, and re-layouts  5.65 us
  transfers between devices with their start and end apart: 1, of which 0 were waited for; matrix products, arithmetic and copies ran while one was open for 8% of the time, Pallas kernels for 0%

commit v1 on v0

v1 whole, which is shorter than its diff:
```python
import functools
import math

import jax
import jax.numpy as jnp
from jax import lax
from jax.experimental import pallas as pl
from jax.experimental.pallas import tpu as pltpu
from jax.sharding import PartitionSpec as P

LAT = 256
ROPE = 64
NOPE_DIM = 128
SPLIT = 4
TOPK = 2
ROWS = 512


def layer_kernel(
    experts, q_hbm, keys_ref, hid_ref, sel_ref, comb_ref, wg_hbm, wu_hbm, wd_hbm,
    att_ref, mix_ref,
    q_v, wg, wu, wd, recv, own, part, cbuf, xbuf, ret, kbuf, acc, m_ref, l_ref,
    local_sem, sz, rz, skz, rkz, sx, rx, skx, rkx, sc, rc, skc, rkc,
    src_, rrc, srx, rrx, srz, rrz,
):
    E = experts
    slots = sel_ref.shape[1]
    toks = keys_ref.shape[0]
    D = hid_ref.shape[1]
    row_total = q_v.shape[0]
    heads = row_total // toks
    width = 512
    me = lax.axis_index("ctx")
    e = me // SPLIT
    s = me % SPLIT
    p = s // 2
    c = s % 2
    s_x = (1 - p) * 2 + c
    dev_x = e * SPLIT + s_x
    dev_c = e * SPLIT + p * 2 + (1 - c)

    def remote(src, dst, ssem, rsem, dev):
        return pltpu.make_async_remote_copy(
            src_ref=src, dst_ref=dst, send_sem=ssem, recv_sem=rsem,
            device_id={"ctx": dev}, device_id_type=pl.DeviceIdType.MESH,
        )

    barrier = pltpu.get_barrier_semaphore()

    def greet(k, _):
        pl.semaphore_signal(
            barrier, inc=1, device_id={"ctx": (e + k) % E * SPLIT + s},
            device_id_type=pl.DeviceIdType.MESH,
        )
        return 0

    lax.fori_loop(1, E, greet, 0)
    for dev in (dev_x, dev_c):
        pl.semaphore_signal(
            barrier, inc=1, device_id={"ctx": dev}, device_id_type=pl.DeviceIdType.MESH
        )
    loads = [
        pltpu.make_async_copy(q_hbm, q_v, local_sem.at[0]),
        pltpu.make_async_copy(wg_hbm, wg, local_sem.at[1]),
        pltpu.make_async_copy(wu_hbm, wu, local_sem.at[2]),
        pltpu.make_async_copy(wd_hbm, wd, local_sem.at[3]),
    ]
    for load in loads:
        load.start()
    kbuf[me] = keys_ref[...]
    pl.semaphore_wait(barrier, E + 1)

    def copy_z(t, i_src):
        return remote(own.at[t], recv.at[me], sz.at[t], rz.at[i_src], t * SPLIT + s)

    def copy_kz(t, i_src):
        return remote(kbuf.at[me], kbuf.at[me], skz.at[t], rkz.at[i_src], t * SPLIT + s)

    def copy_x(g):
        b = g * SPLIT + s
        return remote(recv.at[b], recv.at[b], sx.at[g], rx.at[g], dev_x)

    def copy_kx(g):
        b = g * SPLIT + s
        return remote(kbuf.at[b], kbuf.at[b], skx.at[g], rkx.at[g], dev_x)

    def copy_c(g, far):
        b = g * SPLIT + (s_x if far else s)
        return remote(recv.at[b], recv.at[b], sc.at[2 * g + far], rc.at[2 * g + far], dev_c)

    def copy_kc(g, far):
        b = g * SPLIT + (s_x if far else s)
        return remote(kbuf.at[b], kbuf.at[b], skc.at[2 * g + far], rkc.at[2 * g + far], dev_c)

    def copy_rc(g, q):
        return remote(
            part.at[g * SPLIT + 2 * q + (1 - c)], cbuf.at[2 * g + q],
            src_.at[2 * g + q], rrc.at[2 * g + q], dev_c,
        )

    def copy_rx(g):
        return remote(part.at[g * SPLIT + s_x], xbuf.at[g], srx.at[g], rrx.at[g], dev_x)

    def copy_rz(g, i_src):
        return remote(
            part.at[g * SPLIT + s], ret.at[e], srz.at[g], rrz.at[i_src], g * SPLIT + s
        )

    def dispatch(k, _):
        t = (e + k) % E
        copy_kz(t, e).start()
        own[t] = jnp.dot(
            sel_ref[t], hid_ref[...], preferred_element_type=jnp.float32
        ).astype(jnp.bfloat16)
        copy_z(t, e).start()
        return 0

    lax.fori_loop(1, E, dispatch, 0)
    recv[me] = jnp.dot(
        sel_ref[e], hid_ref[...], preferred_element_type=jnp.float32
    ).astype(jnp.bfloat16)

    def relay(k):
        g = (e + E - k) % E

        @pl.when(k > 0)
        def _():
            copy_kz(g, g).wait_recv()
            copy_z(g, g).wait_recv()

        copy_kx(g).start()
        copy_x(g).start()
        copy_kc(g, 0).start()
        copy_c(g, 0).start()
        copy_kx(g).wait_recv()
        copy_kc(g, 1).start()
        copy_x(g).wait_recv()
        copy_c(g, 1).start()

    def compute(k):
        g = (e + E - k) % E

        @pl.when(k == 0)
        def _():
            for load in loads[1:]:
                load.wait()

        copy_c(g, 0).wait_recv()
        copy_c(g, 1).wait_recv()
        rows = recv[pl.ds(g * SPLIT, SPLIT)].reshape(SPLIT * slots, D)
        gate = jnp.dot(rows, wg[...], preferred_element_type=jnp.float32)
        upper = jnp.dot(rows, wu[...], preferred_element_type=jnp.float32)
        units = (gate / (1.0 + jnp.exp(-gate)) * upper).astype(jnp.bfloat16)
        for start in range(0, D, width):
            piece = jnp.dot(
                units, wd[:, start : start + width], preferred_element_type=jnp.float32
            )
            part[pl.ds(g * SPLIT, SPLIT), :, start : start + width] = piece.astype(
                jnp.bfloat16
            ).reshape(SPLIT, slots, width)
        copy_rc(g, 0).start()
        copy_rc(g, 1).start()

    factor = math.log2(math.e) / math.sqrt(NOPE_DIM + ROPE)

    def attend(k):
        g = (e + E - k) % E
        copy_kc(g, 0).wait_recv()
        copy_kc(g, 1).wait_recv()

        def scores_of(r):
            keys = kbuf[pl.ds(g * SPLIT, SPLIT)].reshape(SPLIT * toks, LAT + ROPE)
            sc_ = lax.dot_general(
                q_v[pl.ds(r, ROWS)], keys, (((1,), (1,)), ((), ())),
                preferred_element_type=jnp.float32,
            )
            return sc_, keys[:, :LAT]

        @pl.when(k == 0)
        def _():
            loads[0].wait()

            def chunk(i, _):
                r = pl.multiple_of(i * ROWS, ROWS)
                sc_, vals = scores_of(r)
                tok = s * toks + (r + lax.broadcasted_iota(jnp.int32, sc_.shape, 0)) // heads
                col = lax.broadcasted_iota(jnp.int32, sc_.shape, 1)
                sc_ = jnp.where(col <= tok, sc_, -jnp.inf)
                m = jnp.max(sc_, axis=1, keepdims=True)
                ex = jnp.exp2((sc_ - m) * factor)
                m_ref[pl.ds(r, ROWS)] = m
                l_ref[pl.ds(r, ROWS)] = jnp.sum(ex, axis=1, keepdims=True)
                acc[pl.ds(r, ROWS)] = jnp.dot(
                    ex.astype(jnp.bfloat16), vals, preferred_element_type=jnp.float32
                )
                return 0

            lax.fori_loop(0, row_total // ROWS, chunk, 0)

        @pl.when(k > 0)
        def _():
            def chunk(i, _):
                r = pl.multiple_of(i * ROWS, ROWS)
                sc_, vals = scores_of(r)
                old = m_ref[pl.ds(r, ROWS)]
                m = jnp.maximum(old, jnp.max(sc_, axis=1, keepdims=True))
                ex = jnp.exp2((sc_ - m) * factor)
                fade = jnp.exp2((old - m) * factor)
                m_ref[pl.ds(r, ROWS)] = m
                l_ref[pl.ds(r, ROWS)] = l_ref[pl.ds(r, ROWS)] * fade + jnp.sum(
                    ex, axis=1, keepdims=True
                )
                acc[pl.ds(r, ROWS)] = acc[pl.ds(r, ROWS)] * fade + jnp.dot(
                    ex.astype(jnp.bfloat16), vals, preferred_element_type=jnp.float32
                )
                return 0

            lax.fori_loop(0, row_total // ROWS, chunk, 0)

        @pl.when(k == e)
        def _():
            def chunk(i, _):
                r = pl.multiple_of(i * ROWS, ROWS)
                att_ref[pl.ds(r, ROWS)] = (
                    acc[pl.ds(r, ROWS)] / l_ref[pl.ds(r, ROWS)]
                ).astype(jnp.bfloat16)
                return 0

            lax.fori_loop(0, row_total // ROWS, chunk, 0)

    def sum_cores(k):
        g = (e + E - k) % E
        copy_rc(g, 0).wait_recv()
        copy_rc(g, 1).wait_recv()
        b = g * SPLIT + s_x
        part[b] = (
            part[b].astype(jnp.float32) + cbuf[2 * g + (1 - p)].astype(jnp.float32)
        ).astype(jnp.bfloat16)
        copy_rx(g).start()

    def sum_chips(k):
        g = (e + E - k) % E
        copy_rx(g).wait_recv()
        b = g * SPLIT + s
        total = (
            part[b].astype(jnp.float32)
            + cbuf[2 * g + p].astype(jnp.float32)
            + xbuf[g].astype(jnp.float32)
        ).astype(jnp.bfloat16)

        @pl.when(k == 0)
        def _():
            ret[e] = total

        @pl.when(k > 0)
        def _():
            part[b] = total
            copy_rz(g, e).start()

    def step(i, _):
        @pl.when(i < E)
        def _():
            relay(i)

        @pl.when((i >= 1) & (i <= E))
        def _():
            compute(i - 1)

        @pl.when((i >= 2) & (i <= E + 1))
        def _():
            sum_cores(i - 2)

        @pl.when((i >= 1) & (i <= e + 1))
        def _():
            attend(i - 1)

        @pl.when(i >= 3)
        def _():
            sum_chips(i - 3)

        return 0

    lax.fori_loop(0, E + 3, step, 0)

    def unread(k, _):
        g = (e + E - k) % E
        copy_kc(g, 0).wait_recv()
        copy_kc(g, 1).wait_recv()
        return 0

    lax.fori_loop(e + 1, E, unread, 0)

    def arrive(k, _):
        g = (e + E - k) % E
        copy_rz(g, g).wait_recv()
        return 0

    lax.fori_loop(1, E, arrive, 0)
    for start in range(0, D, width):
        both = jnp.dot(
            comb_ref[...],
            ret[:, :, start : start + width].reshape(E * slots, width),
            preferred_element_type=jnp.float32,
        )
        mix_ref[:, start : start + width] = (both[:toks] + both[toks:]).astype(jnp.bfloat16)

    def sent(g, _):
        @pl.when(g != e)
        def _():
            copy_kz(g, e).wait_send()
            copy_z(g, e).wait_send()
            copy_rz(g, e).wait_send()

        copy_kx(g).wait_send()
        copy_x(g).wait_send()
        copy_rx(g).wait_send()
        for far in range(2):
            copy_kc(g, far).wait_send()
            copy_c(g, far).wait_send()
            copy_rc(g, far).wait_send()
        return 0

    lax.fori_loop(0, E, sent, 0)


def per_device(queries, latent_keys, hidden, routes, route_weights, w_gate, w_up, w_down):
    toks, heads, qw = queries.shape
    D = hidden.shape[1]
    ff = w_gate.shape[2]
    n_ctx = lax.axis_size("ctx")
    E = n_ctx // SPLIT
    most = toks * TOPK * 5 // (4 * E)
    slots = -(-most // 8) * 8
    flat = routes.reshape(-1)
    ids = jnp.arange(E, dtype=jnp.int32)
    onehot = (flat[:, None] == ids[None, :]).astype(jnp.int32)
    rank = jnp.sum((jnp.cumsum(onehot, axis=0) - onehot) * onehot, axis=1)
    slot = (flat * slots + rank).reshape(toks, TOPK)
    table = jnp.arange(E * slots, dtype=jnp.int32)
    hit = slot[:, :, None] == table[None, None, :]
    sel = (
        jnp.any(slot[None] == table[:, None, None], axis=2)
        .astype(jnp.bfloat16)
        .reshape(E, slots, toks)
    )
    comb = jnp.sum(jnp.where(hit, route_weights[:, :, None], 0.0), axis=1)
    high = lax.reduce_precision(comb, 8, 7)
    comb2 = jnp.concatenate([high, comb - high], axis=0).astype(jnp.bfloat16)
    rows = toks * heads
    bf, f32 = jnp.bfloat16, jnp.float32
    vm = pl.BlockSpec(memory_space=pltpu.VMEM)
    hbm = pl.BlockSpec(memory_space=pl.ANY)
    dma = pltpu.SemaphoreType.DMA
    attended, mixed = pl.pallas_call(
        functools.partial(layer_kernel, E),
        out_shape=(
            jax.ShapeDtypeStruct((rows, LAT), bf),
            jax.ShapeDtypeStruct((toks, D), bf),
        ),
        in_specs=[hbm, vm, vm, vm, vm, hbm, hbm, hbm],
        out_specs=(vm, vm),
        scratch_shapes=[
            pltpu.VMEM((rows, qw), bf),
            pltpu.VMEM((D, ff), bf),
            pltpu.VMEM((D, ff), bf),
            pltpu.VMEM((ff, D), bf),
            pltpu.VMEM((n_ctx, slots, D), bf),
            pltpu.VMEM((E, slots, D), bf),
            pltpu.VMEM((n_ctx, slots, D), bf),
            pltpu.VMEM((2 * E, slots, D), bf),
            pltpu.VMEM((E, slots, D), bf),
            pltpu.VMEM((E, slots, D), bf),
            pltpu.VMEM((n_ctx, toks, qw), bf),
            pltpu.VMEM((rows, LAT), f32),
            pltpu.VMEM((rows, 1), f32),
            pltpu.VMEM((rows, 1), f32),
            dma((4,)),
        ]
        + [dma((E,))] * 8
        + [dma((2 * E,))] * 6
        + [dma((E,))] * 4,
        compiler_params=pltpu.CompilerParams(
            collective_id=0, has_side_effects=True, vmem_limit_bytes=60 * 1024 * 1024
        ),
    )(
        queries.reshape(rows, qw), latent_keys, hidden, sel, comb2,
        w_gate[0], w_up[0], w_down[0],
    )
    return (attended.reshape(toks, heads, LAT), mixed)


def solution(mesh):
    in_specs = (
        P(("group", "ctx"), None, None),
        P(("group", "ctx"), None),
        P(("group", "ctx"), None),
        P(("group", "ctx"), None),
        P(("group", "ctx"), None),
        P("ctx", None, None),
        P("ctx", None, None),
        P("ctx", None, None),
    )
    out_specs = (P(("group", "ctx"), None, None), P(("group", "ctx"), None))
    return jax.shard_map(
        per_device, mesh=mesh, in_specs=in_specs, out_specs=out_specs, check_vma=False
    )
```

time: 279 us -> 120 us (0.43)
  the two profiles are of different devices: /device:TPU:17 before, /device:TPU:0 now
where the time goes in v1:
time: 120 us; the launch traced here: 119 us
  Pallas kernels  110 us (92%)
  local copies, waits for them, and re-layouts  5.82 us (5%)
  other arithmetic  2.66 us (2%)
    pallas_call x1, Pallas kernels, per_device(): pl.pallas_call(functools.partial(layer_kernel, E), out_shape=(jax.ShapeDt...  110 us
    unnamed x5, local copies, waits for them, and re-layouts  4.75 us

profile of v1, /device:TPU:0, one launch (start us, length us, event | category | flops | bytes accessed | tf_op | source)
XLA Modules:
  0.0 119.5 jit_solution(9734632209003428532)
XLA Ops:
  0.6 0.8 copy.24
  1.4 0.1 eq.20
  1.5 0.1 fusion.2
  1.6 0.2 reduce_window_sum.11
  1.8 0.2 select_reduce_fusion.1
  2.0 0.1 reduce_sum.21
  2.1 0.1 copy.25
  2.2 0.7 multiply_add_fusion
  2.9 0.1 fusion
  3.0 0.7 copy.26
  3.7 0.8 select_reduce_fusion
  4.5 0.6 pad_maximum_fusion.comb_ref
  5.2 110.3 %shard_map.95 = (bf16[4096,256]{1,0:T(8,128)(2,1)}, bf16[64,3584]{1,0:T(8,128)(2,1)}) custom-call(bf16[4096,320]{1,0:T(8,128)(2,1)} %bitcast.6, bf16[64,320]{1,0:T(8,128)(2,1)} %keys_ref.1, bf16[64,3584]{1,0:T(8,128)(2,1)} %hid_ref.1, bf16[4,40,64]{2,1,0:T(8,128)(2,1)} %bitcast.11, bf16[128,160]{1,0:T(8,128)(2,1)} %pad_maximum_fusion.comb_ref, ...), custom_call_target="tpu_custom_call" | custom-call | tf_op jit(solution)/shard_map/pallas_call | solution.py:354
  115.5 0.0 copy-start
  115.5 3.2 %copy.29 = bf16[64,64,256]{2,1,0:T(8,128)(2,1)} copy(bf16[64,64,256]{2,1,0:T(8,128)(2,1)} %bitcast.7) | data formatting | bytes 4194304
  118.7 0.0 copy-done
  118.7 0.8 copy.30
  (2 shorter events, 0.0 us)
Async XLA Ops:
  115.5 3.2 %copy-start = (bf16[64,3584]{1,0:T(8,128)(2,1)S(1)}, bf16[64,3584]{1,0:T(8,128)(2,1)}, u32[]{:S(2)}) copy-start(bf16[64,3584]{1,0:T(8,128)(2,1)} %get-tuple-element.11) | copy-start | bytes 1376260

commit v2 on v1

v2 whole, which is shorter than its diff:
```python
import functools
import math

import jax
import jax.numpy as jnp
from jax import lax
from jax.experimental import pallas as pl
from jax.experimental.pallas import tpu as pltpu
from jax.sharding import PartitionSpec as P

LAT = 256
ROPE = 64
NOPE_DIM = 128
SPLIT = 4
TOPK = 2
ROWS = 512


PARTS = 2
AHEAD = 1


def layer_kernel(
    experts, slots, q_hbm, keys_ref, hid_ref, routes_ref, routes_t_ref, weights_ref,
    wg_hbm, wu_hbm, wd_hbm,
    att_ref, mix_ref,
    q_v, wg, wu, wd, recv, own, part, cbuf, xbuf, ret, kbuf, acc, m_ref, l_ref,
    local_sem, sz, rz, sx, rx, srx, rrx, srz, rrz, sc, rc, src_, rrc,
    skz, rkz, skx, rkx, skc, rkc,
):
    E = experts
    toks = keys_ref.shape[0]
    D = hid_ref.shape[1]
    dh = D // PARTS
    row_total = q_v.shape[0]
    heads = row_total // toks
    me = lax.axis_index("ctx")
    e = me // SPLIT
    s = me % SPLIT
    p = s // 2
    c = s % 2
    s_x = (1 - p) * 2 + c
    dev_x = e * SPLIT + s_x
    dev_c = e * SPLIT + p * 2 + (1 - c)

    def remote(src, dst, ssem, rsem, dev):
        return pltpu.make_async_remote_copy(
            src_ref=src, dst_ref=dst, send_sem=ssem, recv_sem=rsem,
            device_id={"ctx": dev}, device_id_type=pl.DeviceIdType.MESH,
        )

    barrier = pltpu.get_barrier_semaphore()

    def greet(k, _):
        pl.semaphore_signal(
            barrier, inc=1, device_id={"ctx": (e + k) % E * SPLIT + s},
            device_id_type=pl.DeviceIdType.MESH,
        )
        return 0

    lax.fori_loop(1, E, greet, 0)
    for dev in (dev_x, dev_c):
        pl.semaphore_signal(
            barrier, inc=1, device_id={"ctx": dev}, device_id_type=pl.DeviceIdType.MESH
        )
    loads = [
        pltpu.make_async_copy(q_hbm, q_v, local_sem.at[0]),
        pltpu.make_async_copy(wg_hbm, wg, local_sem.at[1]),
        pltpu.make_async_copy(wu_hbm, wu, local_sem.at[2]),
        pltpu.make_async_copy(wd_hbm, wd, local_sem.at[3]),
    ]
    for load in loads:
        load.start()
    kbuf[me] = keys_ref[...]

    older = lax.broadcasted_iota(jnp.int32, (toks, toks), 1)
    newer = lax.broadcasted_iota(jnp.int32, (toks, toks), 0)
    slot_col, slot_row = [], []
    for k in range(TOPK):
        col_id, row_id = routes_ref[:, k : k + 1], routes_t_ref[k : k + 1, :]
        col_rank = jnp.zeros((toks, 1), jnp.int32)
        row_rank = jnp.zeros((1, toks), jnp.int32)
        for j in range(TOPK):
            before = (routes_t_ref[j : j + 1, :] == col_id) & (
                older * TOPK + j < newer * TOPK + k
            )
            col_rank += jnp.sum(before.astype(jnp.int32), axis=1, keepdims=True)
            before = (routes_ref[:, j : j + 1] == row_id) & (
                newer * TOPK + j < older * TOPK + k
            )
            row_rank += jnp.sum(before.astype(jnp.int32), axis=0, keepdims=True)
        slot_col.append(col_id * slots + col_rank)
        slot_row.append(row_id * slots + row_rank)

    def select(t):
        place = t * slots + lax.broadcasted_iota(jnp.int32, (slots, toks), 0)
        hit = jnp.where(place == slot_row[0], 1.0, 0.0)
        for k in range(1, TOPK):
            hit += jnp.where(place == slot_row[k], 1.0, 0.0)
        return hit.astype(jnp.bfloat16)

    pl.semaphore_wait(barrier, E + 1)

    def copy_z(t, i_src, h):
        return remote(
            own.at[h, t], recv.at[h, me], sz.at[h, t], rz.at[h, i_src], t * SPLIT + s
        )

    def copy_kz(t, i_src):
        return remote(kbuf.at[me], kbuf.at[me], skz.at[t], rkz.at[i_src], t * SPLIT + s)

    def copy_x(g, h):
        b = g * SPLIT + s
        return remote(recv.at[h, b], recv.at[h, b], sx.at[h, g], rx.at[h, g], dev_x)

    def copy_kx(g):
        b = g * SPLIT + s
        return remote(kbuf.at[b], kbuf.at[b], skx.at[g], rkx.at[g], dev_x)

    def copy_c(g, far, h):
        b = g * SPLIT + (s_x if far else s)
        return remote(
            recv.at[h, b], recv.at[h, b], sc.at[h, 2 * g + far], rc.at[h, 2 * g + far], dev_c
        )

    def copy_kc(g, far):
        b = g * SPLIT + (s_x if far else s)
        return remote(kbuf.at[b], kbuf.at[b], skc.at[2 * g + far], rkc.at[2 * g + far], dev_c)

    def copy_rc(g, q, h):
        return remote(
            part.at[h, g * SPLIT + 2 * q + (1 - c)], cbuf.at[h, 2 * g + q],
            src_.at[h, 2 * g + q], rrc.at[h, 2 * g + q], dev_c,
        )

    def copy_rx(g, h):
        return remote(
            part.at[h, g * SPLIT + s_x], xbuf.at[h, g], srx.at[h, g], rrx.at[h, g], dev_x
        )

    def copy_rz(g, i_src, h):
        return remote(
            part.at[h, g * SPLIT + s], ret.at[h, e], srz.at[h, g], rrz.at[h, i_src],
            g * SPLIT + s,
        )

    def send_keys(k, _):
        copy_kz((e + k) % E, e).start()
        return 0

    lax.fori_loop(1, E, send_keys, 0)
    copy_kx(e).start()
    copy_kc(e, 0).start()

    def dispatch(k):
        t = (e + k) % E
        mine = select(t)
        for h in range(PARTS):
            own[h, t] = jnp.dot(
                mine, hid_ref[:, h * dh : (h + 1) * dh], preferred_element_type=jnp.float32
            ).astype(jnp.bfloat16)
            copy_z(t, e, h).start()

    @pl.when(E > 1)
    def _():
        dispatch(1)

    mine = select(e)
    for h in range(PARTS):
        recv[h, me] = jnp.dot(
            mine, hid_ref[:, h * dh : (h + 1) * dh], preferred_element_type=jnp.float32
        ).astype(jnp.bfloat16)
        copy_x(e, h).start()
        copy_c(e, 0, h).start()

    def early(k, _):
        dispatch(k)
        return 0

    lax.fori_loop(2, min(E, 1 + AHEAD), early, 0)

    def source(k):
        return (e + E - k) % E

    def relay_near(k):
        g = source(k)
        for h in range(PARTS):
            copy_z(g, g, h).wait_recv()
            copy_x(g, h).start()
            copy_c(g, 0, h).start()

        @pl.when(k + AHEAD < E)
        def _():
            dispatch(k + AHEAD)

    def relay_far(k):
        g = source(k)
        for h in range(PARTS):
            copy_x(g, h).wait_recv()
            copy_c(g, 1, h).start()

    def compute(k):
        g = source(k)

        @pl.when(k == 0)
        def _():
            for load in loads[1:]:
                load.wait()

        gate = jnp.zeros((SPLIT * slots, wg.shape[1]), jnp.float32)
        upper = gate
        for h in range(PARTS):
            copy_c(g, 0, h).wait_recv()
            copy_c(g, 1, h).wait_recv()
            rows = recv[h, pl.ds(g * SPLIT, SPLIT)].reshape(SPLIT * slots, dh)
            cut = slice(h * dh, (h + 1) * dh)
            gate += jnp.dot(rows, wg[cut, :], preferred_element_type=jnp.float32)
            upper += jnp.dot(rows, wu[cut, :], preferred_element_type=jnp.float32)
        units = (gate / (1.0 + jnp.exp(-gate)) * upper).astype(jnp.bfloat16)
        width = dh // 2
        for h in range(PARTS):
            for start in range(0, dh, width):
                piece = jnp.dot(
                    units, wd[:, h * dh + start : h * dh + start + width],
                    preferred_element_type=jnp.float32,
                )
                part[h, pl.ds(g * SPLIT, SPLIT), :, start : start + width] = piece.astype(
                    jnp.bfloat16
                ).reshape(SPLIT, slots, width)
            copy_rc(g, 1 - p, h).start()
            copy_rc(g, p, h).start()

    factor = math.log2(math.e) / math.sqrt(NOPE_DIM + ROPE)

    def attend(k):
        g = source(k)
        copy_kc(g, 0).wait_recv()
        copy_kc(g, 1).wait_recv()

        def scores_of(r):
            keys = kbuf[pl.ds(g * SPLIT, SPLIT)].reshape(SPLIT * toks, LAT + ROPE)
            sc_ = lax.dot_general(
                q_v[pl.ds(r, ROWS)], keys, (((1,), (1,)), ((), ())),
                preferred_element_type=jnp.float32,
            )
            return sc_, keys[:, :LAT]

        @pl.when(k == 0)
        def _():
            loads[0].wait()

            def chunk(i, _):
                r = pl.multiple_of(i * ROWS, ROWS)
                sc_, vals = scores_of(r)
                tok = s * toks + (r + lax.broadcasted_iota(jnp.int32, sc_.shape, 0)) // heads
                col = lax.broadcasted_iota(jnp.int32, sc_.shape, 1)
                sc_ = jnp.where(col <= tok, sc_, -jnp.inf)
                m = jnp.max(sc_, axis=1, keepdims=True)
                ex = jnp.exp2((sc_ - m) * factor)
                m_ref[pl.ds(r, ROWS)] = m
                l_ref[pl.ds(r, ROWS)] = jnp.sum(ex, axis=1, keepdims=True)
                acc[pl.ds(r, ROWS)] = jnp.dot(
                    ex.astype(jnp.bfloat16), vals, preferred_element_type=jnp.float32
                )
                return 0

            lax.fori_loop(0, row_total // ROWS, chunk, 0)

        @pl.when(k > 0)
        def _():
            def chunk(i, _):
                r = pl.multiple_of(i * ROWS, ROWS)
                sc_, vals = scores_of(r)
                old = m_ref[pl.ds(r, ROWS)]
                m = jnp.maximum(old, jnp.max(sc_, axis=1, keepdims=True))
                ex = jnp.exp2((sc_ - m) * factor)
                fade = jnp.exp2((old - m) * factor)
                m_ref[pl.ds(r, ROWS)] = m
                l_ref[pl.ds(r, ROWS)] = l_ref[pl.ds(r, ROWS)] * fade + jnp.sum(
                    ex, axis=1, keepdims=True
                )
                acc[pl.ds(r, ROWS)] = acc[pl.ds(r, ROWS)] * fade + jnp.dot(
                    ex.astype(jnp.bfloat16), vals, preferred_element_type=jnp.float32
                )
                return 0

            lax.fori_loop(0, row_total // ROWS, chunk, 0)

    def sum_cores(k):
        g = source(k)
        b = g * SPLIT + s_x
        for h in range(PARTS):
            copy_rc(g, 1 - p, h).wait_recv()
            part[h, b] = (
                part[h, b].astype(jnp.float32)
                + cbuf[h, 2 * g + (1 - p)].astype(jnp.float32)
            ).astype(jnp.bfloat16)
            copy_rx(g, h).start()

    def sum_chips(k):
        g = source(k)
        b = g * SPLIT + s
        for h in range(PARTS):
            copy_rc(g, p, h).wait_recv()
            copy_rx(g, h).wait_recv()
            total = (
                part[h, b].astype(jnp.float32)
                + cbuf[h, 2 * g + p].astype(jnp.float32)
                + xbuf[h, g].astype(jnp.float32)
            ).astype(jnp.bfloat16)

            @pl.when(k == 0)
            def _():
                ret[h, e] = total

            @pl.when(k > 0)
            def _():
                part[h, b] = total
                copy_rz(g, e, h).start()

    def relay_keys(k, _):
        g = source(k)

        @pl.when(k > 0)
        def _():
            copy_kz(g, g).wait_recv()
            copy_kx(g).start()
            copy_kc(g, 0).start()

        copy_kx(g).wait_recv()
        copy_kc(g, 1).start()
        return 0

    lax.fori_loop(0, E, relay_keys, 0)
    relay_far(0)
    attend(0)
    compute(0)

    def step(k, _):
        relay_near(k)
        sum_cores(k - 1)

        @pl.when(k <= e)
        def _():
            attend(k)

        relay_far(k)
        sum_chips(k - 1)
        compute(k)
        return 0

    lax.fori_loop(1, E, step, 0)
    sum_cores(E - 1)
    sum_chips(E - 1)

    def finish(i, _):
        r = pl.multiple_of(i * ROWS, ROWS)
        att_ref[pl.ds(r, ROWS)] = (acc[pl.ds(r, ROWS)] / l_ref[pl.ds(r, ROWS)]).astype(
            jnp.bfloat16
        )
        return 0

    lax.fori_loop(0, row_total // ROWS, finish, 0)

    def unread(k, _):
        g = source(k)
        copy_kc(g, 0).wait_recv()
        copy_kc(g, 1).wait_recv()
        return 0

    lax.fori_loop(e + 1, E, unread, 0)

    def sent(g, _):
        @pl.when(g != e)
        def _():
            copy_kz(g, e).wait_send()
            for h in range(PARTS):
                copy_z(g, e, h).wait_send()

        copy_kx(g).wait_send()
        for far in range(2):
            copy_kc(g, far).wait_send()
        for h in range(PARTS):
            copy_x(g, h).wait_send()
            copy_rx(g, h).wait_send()
            for far in range(2):
                copy_c(g, far, h).wait_send()
                copy_rc(g, far, h).wait_send()
        return 0

    lax.fori_loop(0, E, sent, 0)

    place = lax.broadcasted_iota(jnp.int32, (toks, E * slots), 1)
    comb = jnp.where(place == slot_col[0], weights_ref[:, 0:1], 0.0)
    for k in range(1, TOPK):
        comb += jnp.where(place == slot_col[k], weights_ref[:, k : k + 1], 0.0)
    high = comb.astype(jnp.bfloat16)
    low = (comb - high.astype(jnp.float32)).astype(jnp.bfloat16)
    both = jnp.concatenate([high, low], axis=0)
    for h in range(PARTS):

        def arrive(k, _):
            g = source(k)
            copy_rz(g, g, h).wait_recv()
            return 0

        lax.fori_loop(1, E, arrive, 0)
        out = jnp.dot(
            both, ret[h].reshape(E * slots, dh), preferred_element_type=jnp.float32
        )
        mix_ref[:, h * dh : (h + 1) * dh] = (out[:toks] + out[toks:]).astype(jnp.bfloat16)

    def returned(g, _):
        @pl.when(g != e)
        def _():
            for h in range(PARTS):
                copy_rz(g, e, h).wait_send()

        return 0

    lax.fori_loop(0, E, returned, 0)


def per_device(queries, latent_keys, hidden, routes, route_weights, w_gate, w_up, w_down):
    toks, heads, qw = queries.shape
    D = hidden.shape[1]
    ff = w_gate.shape[2]
    n_ctx = lax.axis_size("ctx")
    E = n_ctx // SPLIT
    most = toks * TOPK * 5 // (4 * E)
    slots = -(-most // 8) * 8
    rows = toks * heads
    dh = D // PARTS
    bf, f32 = jnp.bfloat16, jnp.float32
    vm = pl.BlockSpec(memory_space=pltpu.VMEM)
    hbm = pl.BlockSpec(memory_space=pl.ANY)
    dma = pltpu.SemaphoreType.DMA
    attended, mixed = pl.pallas_call(
        functools.partial(layer_kernel, E, slots),
        out_shape=(
            jax.ShapeDtypeStruct((rows, LAT), bf),
            jax.ShapeDtypeStruct((toks, D), bf),
        ),
        in_specs=[hbm, vm, vm, vm, vm, vm, hbm, hbm, hbm],
        out_specs=(vm, vm),
        scratch_shapes=[
            pltpu.VMEM((rows, qw), bf),
            pltpu.VMEM((D, ff), bf),
            pltpu.VMEM((D, ff), bf),
            pltpu.VMEM((ff, D), bf),
            pltpu.VMEM((PARTS, n_ctx, slots, dh), bf),
            pltpu.VMEM((PARTS, E, slots, dh), bf),
            pltpu.VMEM((PARTS, n_ctx, slots, dh), bf),
            pltpu.VMEM((PARTS, 2 * E, slots, dh), bf),
            pltpu.VMEM((PARTS, E, slots, dh), bf),
            pltpu.VMEM((PARTS, E, slots, dh), bf),
            pltpu.VMEM((n_ctx, toks, qw), bf),
            pltpu.VMEM((rows, LAT), f32),
            pltpu.VMEM((rows, 1), f32),
            pltpu.VMEM((rows, 1), f32),
            dma((4,)),
        ]
        + [dma((PARTS, E))] * 8
        + [dma((PARTS, 2 * E))] * 4
        + [dma((E,))] * 4
        + [dma((2 * E,))] * 2,
        compiler_params=pltpu.CompilerParams(
            collective_id=0, has_side_effects=True, vmem_limit_bytes=60 * 1024 * 1024
        ),
    )(
        queries.reshape(rows, qw), latent_keys, hidden, routes, routes.T, route_weights,
        w_gate[0], w_up[0], w_down[0],
    )
    return (attended.reshape(toks, heads, LAT), mixed)


def solution(mesh):
    in_specs = (
        P(("group", "ctx"), None, None),
        P(("group", "ctx"), None),
        P(("group", "ctx"), None),
        P(("group", "ctx"), None),
        P(("group", "ctx"), None),
        P("ctx", None, None),
        P("ctx", None, None),
        P("ctx", None, None),
    )
    out_specs = (P(("group", "ctx"), None, None), P(("group", "ctx"), None))
    return jax.shard_map(
        per_device, mesh=mesh, in_specs=in_specs, out_specs=out_specs, check_vma=False
    )
```

time: 120 us -> 100 us (0.83)
  Pallas kernels: 110 us -> 92.9 us
  other arithmetic: 2.66 us -> 0 us
    pallas_call x1, Pallas kernels: 110 us -> 92.9 us  [per_device(): pl.pallas_call(functools.partial(layer_kernel, E, slots), out_shape=(jax....]
    unnamed x5 -> x6, local copies, waits for them, and re-layouts: 4.75 us -> 6.75 us
where the time goes in v2:
time: 100 us
  Pallas kernels  92.9 us (93%)
  local copies, waits for them, and re-layouts  6.75 us (7%)
    pallas_call x1, Pallas kernels, per_device(): pl.pallas_call(functools.partial(layer_kernel, E, slots), out_shape=(jax....  92.9 us
    unnamed x6, local copies, waits for them, and re-layouts  6.75 us

profile of v2, /device:TPU:0, one launch (start us, length us, event | category | flops | bytes accessed | tf_op | source)
XLA Modules:
  0.0 100.2 jit_solution(17416127591228701905)
XLA Ops:
  0.6 1.4 %copy.11.weights_ref = f32[64,2]{1,0:T(8,128)} copy(f32[64,2]{0,1:T(2,128)} %param.12) | data formatting | bytes 1024 | tf_op args[4]
  2.0 1.4 %copy.10.routes_ref = s32[64,2]{1,0:T(8,128)} copy(s32[64,2]{0,1:T(2,128)} %param.11) | data formatting | bytes 1024 | tf_op args[3]
  3.4 92.9 %shard_map.95 = (bf16[4096,256]{1,0:T(8,128)(2,1)}, bf16[64,3584]{1,0:T(8,128)(2,1)}) custom-call(bf16[4096,320]{1,0:T(8,128)(2,1)} %bitcast.6, bf16[64,320]{1,0:T(8,128)(2,1)} %keys_ref.1, bf16[64,3584]{1,0:T(8,128)(2,1)} %hid_ref.1, s32[64,2]{1,0:T(8,128)} %copy.10.routes_ref, s32[2,64]{1,0:T(2,128)} %bitcast.11, f32[64,2]{1,0:T(8,128)} %copy.11.weights_ref, ...), custom_call_target="tpu_custom_call" | custom-call | tf_op jit(solution)/shard_map/pallas_call | solution.py:438
  96.3 0.0 copy-start
  96.3 3.2 %copy.14 = bf16[64,64,256]{2,1,0:T(8,128)(2,1)} copy(bf16[64,64,256]{2,1,0:T(8,128)(2,1)} %bitcast.7) | data formatting | bytes 4194304
  99.5 0.0 copy-done
  99.5 0.8 copy.15
Async XLA Ops:
  96.3 3.2 %copy-start = (bf16[64,3584]{1,0:T(8,128)(2,1)S(1)}, bf16[64,3584]{1,0:T(8,128)(2,1)}, u32[]{:S(2)}) copy-start(bf16[64,3584]{1,0:T(8,128)(2,1)} %get-tuple-element.9) | copy-start | bytes 1376260

commit v3 on v2

--- a/solution.py
+++ b/solution.py
@@ -338,15 +338,15 @@
 
     def step(k, _):
         relay_near(k)
+
+        @pl.when(k <= e)
+        def _():
+            attend(k)
+
+        relay_far(k)
         sum_cores(k - 1)
-
-        @pl.when(k <= e)
-        def _():
-            attend(k)
-
-        relay_far(k)
+        compute(k)
         sum_chips(k - 1)
-        compute(k)
         return 0
 
     lax.fori_loop(1, E, step, 0)

time: 100 us -> 105 us (1.050)
  Pallas kernels: 92.9 us -> 97.3 us
    pallas_call x1, Pallas kernels: 92.9 us -> 97.3 us  [per_device(): pl.pallas_call(functools.partial(layer_kernel, E, slots), out_shape=(jax....]
where the time goes in v3:
time: 105 us
  Pallas kernels  97.3 us (93%)
  local copies, waits for them, and re-layouts  6.75 us (6%)
    pallas_call x1, Pallas kernels, per_device(): pl.pallas_call(functools.partial(layer_kernel, E, slots), out_shape=(jax....  97.3 us
    unnamed x6, local copies, waits for them, and re-layouts  6.75 us

profile of v3, /device:TPU:0, one launch (start us, length us, event | category | flops | bytes accessed | tf_op | source)
XLA Modules:
  0.0 104.7 jit_solution(8152015695637699788)
XLA Ops:
  0.6 1.4 %copy.11.weights_ref = f32[64,2]{1,0:T(8,128)} copy(f32[64,2]{0,1:T(2,128)} %param.12) | data formatting | bytes 1024 | tf_op args[4]
  2.0 1.4 %copy.10.routes_ref = s32[64,2]{1,0:T(8,128)} copy(s32[64,2]{0,1:T(2,128)} %param.11) | data formatting | bytes 1024 | tf_op args[3]
  3.4 97.3 %shard_map.95 = (bf16[4096,256]{1,0:T(8,128)(2,1)}, bf16[64,3584]{1,0:T(8,128)(2,1)}) custom-call(bf16[4096,320]{1,0:T(8,128)(2,1)} %bitcast.6, bf16[64,320]{1,0:T(8,128)(2,1)} %keys_ref.1, bf16[64,3584]{1,0:T(8,128)(2,1)} %hid_ref.1, s32[64,2]{1,0:T(8,128)} %copy.10.routes_ref, s32[2,64]{1,0:T(2,128)} %bitcast.11, f32[64,2]{1,0:T(8,128)} %copy.11.weights_ref, ...), custom_call_target="tpu_custom_call" | custom-call | tf_op jit(solution)/shard_map/pallas_call | solution.py:438
  100.7 0.0 copy-start
  100.8 3.2 %copy.14 = bf16[64,64,256]{2,1,0:T(8,128)(2,1)} copy(bf16[64,64,256]{2,1,0:T(8,128)(2,1)} %bitcast.7) | data formatting | bytes 4194304
  104.0 0.0 copy-done
  104.0 0.8 copy.15
Async XLA Ops:
  100.7 3.2 %copy-start = (bf16[64,3584]{1,0:T(8,128)(2,1)S(1)}, bf16[64,3584]{1,0:T(8,128)(2,1)}, u32[]{:S(2)}) copy-start(bf16[64,3584]{1,0:T(8,128)(2,1)} %get-tuple-element.9) | copy-start | bytes 1376260
